TPU v7x, 512 devices: a whole 4x8x8 slice. The times are simulated.
512 devices in a mesh: ctx: 64 (over x, z, core), tp: 8 (over y).
Axes of the slice: x: 4, y: 8, z: 8, core: 2. Of those that a mesh axis runs over, the one named last changes fastest.
Arguments:
- features: bfloat16 [128, 196, 1152], P('ctx', None, 'tp'), may hold values from -6 to 6
- group_kernel: bfloat16 [9, 1152, 48], P(None, 'tp'), may hold values from -0.3125 to 0.3125
- squeeze_in: bfloat16 [1152, 288], P('tp'), may hold values from -0.75 to 0.75
- squeeze_out: bfloat16 [288, 1152], P(None, 'tp'), may hold values from -0.75 to 0.75
- sampler_kernel: bfloat16 [1152, 8, 1152], P('ctx', None, 'tp'), may hold values from -0.0625 to 0.0625
- readout_kernel: bfloat16 [1152, 8192], P('ctx', 'tp'), may hold values from -0.1875 to 0.1875
- frame_clip: int32 [128], replicated, may hold values from 0 to 15, as said below
- clip_keep: int32 [16], replicated, may hold values from 1 to 512, as said below
- token_cotangent: bfloat16 [4096, 8192], P('ctx', 'tp'), may hold values from -6 to 6
Outputs:
- llm_tokens: bfloat16 [4096, 8192], P('ctx', 'tp')
- grad_features: bfloat16 [128, 196, 1152], P('ctx', None, 'tp')
Inputs may be any that keep to these rules, and one draw needn't show every extreme that they name: `frame_clip`: clip ids start at 0 and never fall along the frames; every clip covers an even number of frames from 2 to 16 and starts at an even frame; some clip covers 16. `clip_keep`: each clip keeps at least one and at most 8 * 8 times half its frames of its tokens; the clip of 16 frames keeps all of its tokens, and some clip keeps a single token.
All inputs are finite; a program needn't handle non-finite values.
Results may differ from a plain program's by a relative error of at most 0.009.
Values may be sent and summed in bfloat16 or wider, within the bound.
A program may use at most 64 MiB of HBM per device.

v0:
```python
import jax
import jax.numpy as jnp
from jax import lax
from jax.sharding import PartitionSpec as P

SIDE = 14
OUT_SIDE = 8


def shifted(value, axis, by):
    count = lax.axis_size(axis)
    pairs = [(i, i + by) for i in range(count) if 0 <= i + by < count]
    return lax.ppermute(value, axis, pairs)


def silu_slope(values):
    sigma = jax.nn.sigmoid(values)
    return sigma * (1.0 + values * (1.0 - sigma))


def grouped_forward(frames_grid, group_kernel):
    count, side, _, chans = frames_grid.shape
    width = group_kernel.shape[2]
    groups = chans // width
    padded = jnp.pad(frames_grid, ((0, 0), (1, 1), (1, 1), (0, 0)))
    kernel = group_kernel.reshape(9, groups, width, width)
    total = jnp.zeros((count, side, side, groups, width), jnp.float32)
    for kernel_tap in range(9):
        row_shift, col_shift = divmod(kernel_tap, 3)
        window = padded[:, row_shift : row_shift + side, col_shift : col_shift + side]
        window = window.reshape(count, side, side, groups, width)
        total = total + jnp.einsum(
            "fyxgi,gio->fyxgo", window, kernel[kernel_tap], preferred_element_type=jnp.float32
        )
    return total.reshape(count, side, side, chans)


def grouped_backward(grad_grid, group_kernel):
    count, side, _, chans = grad_grid.shape
    width = group_kernel.shape[2]
    groups = chans // width
    kernel = group_kernel.reshape(9, groups, width, width)
    source = grad_grid.reshape(count, side, side, groups, width)
    total = jnp.zeros((count, side + 2, side + 2, chans), jnp.float32)
    for kernel_tap in range(9):
        row_shift, col_shift = divmod(kernel_tap, 3)
        spread = jnp.einsum(
            "fyxgo,gio->fyxgi", source, kernel[kernel_tap], preferred_element_type=jnp.float32
        )
        spread = spread.reshape(count, side, side, chans)
        total = total + jnp.pad(
            spread, ((0, 0), (row_shift, 2 - row_shift), (col_shift, 2 - col_shift), (0, 0))
        )
    return total[:, 1 : side + 1, 1 : side + 1]


def make_patches(prev_odd, even):
    stacked = jnp.stack([prev_odd, even], axis=1)
    stacked = jnp.pad(stacked, ((0, 0), (0, 0), (1, 1), (1, 1), (0, 0)))
    pairs, _, padded_side, _, chans = stacked.shape
    half = padded_side // 2
    shaped = stacked.reshape(pairs, 2, half, 2, half, 2, chans).transpose(0, 2, 4, 1, 3, 5, 6)
    return shaped.reshape(pairs * half * half, 8 * chans)


def unpatch(grad_rows, pairs, side, chans):
    half = side // 2 + 1
    shaped = grad_rows.reshape(pairs, half, half, 2, 2, 2, chans).transpose(0, 3, 1, 4, 2, 5, 6)
    shaped = shaped.reshape(pairs, 2, 2 * half, 2 * half, chans)
    return shaped[:, :, 1 : side + 1, 1 : side + 1]


def contract_last(left, right):
    return lax.dot_general(
        left, right, (((1,), (1,)), ((), ())), preferred_element_type=jnp.float32
    )


def per_device(
    features,
    group_kernel,
    squeeze_in,
    squeeze_out,
    sampler_kernel,
    readout_kernel,
    frame_clip,
    clip_keep,
    token_cotangent,
):
    highest = lax.Precision.HIGHEST
    shard_index = lax.axis_index("ctx")
    frames_dev, cells, chans = features.shape
    pairs_dev = frames_dev // 2
    grid = features.reshape(frames_dev, SIDE, SIDE, chans)
    conv_out = grouped_forward(grid, group_kernel)
    active = jax.nn.silu(conv_out)
    pooled = jnp.mean(active, axis=(1, 2))
    squeezed = lax.psum(jnp.dot(pooled, squeeze_in.astype(jnp.float32), precision=highest), "tp")
    relaxed = jax.nn.silu(squeezed)
    excite = jax.nn.sigmoid(jnp.dot(relaxed, squeeze_out.astype(jnp.float32), precision=highest))
    hidden = (grid.astype(jnp.float32) + active * excite[:, None, None, :]).astype(jnp.bfloat16)
    full_sampler, full_readout = (
        lax.all_gather(sampler_kernel, "ctx", axis=0, tiled=True),
        lax.all_gather(readout_kernel, "ctx", axis=0, tiled=True),
    )
    sampler_rows = full_sampler.reshape(full_sampler.shape[0], 8 * chans)
    halo_frame = shifted(hidden[-1], "ctx", 1)
    local_clip = lax.dynamic_slice_in_dim(frame_clip, shard_index * frames_dev, frames_dev)
    edge_clip = lax.dynamic_slice_in_dim(
        frame_clip, jnp.maximum(shard_index * frames_dev - 1, 0), 1
    )
    first_keep = jnp.logical_and(shard_index > 0, edge_clip[0] == local_clip[0])
    later_keep = local_clip[1:-1:2] == local_clip[2::2]
    pair_mask = jnp.concatenate([first_keep[None], later_keep]).astype(jnp.float32)
    even = hidden[0::2]
    odd = hidden[1::2]
    prev_odd = jnp.concatenate([halo_frame[None], odd[:-1]], axis=0)
    prev_odd = prev_odd * pair_mask.astype(jnp.bfloat16)[:, None, None, None]
    patches = make_patches(prev_odd, even)
    per_frame = OUT_SIDE * OUT_SIDE
    pair_clip = frame_clip[0::2]
    clip_ids = jnp.arange(clip_keep.shape[0], dtype=jnp.int32)
    start_pair = jnp.sum((pair_clip[None, :] < clip_ids[:, None]).astype(jnp.int32), axis=1)
    own_clip = local_clip[0::2]
    one_hot = (own_clip[:, None] == clip_ids[None, :]).astype(jnp.int32)
    own_start = jnp.sum(one_hot * start_pair[None, :], axis=1)
    own_keep = jnp.sum(one_hot * clip_keep[None, :], axis=1)
    pair_index = shard_index * pairs_dev + jnp.arange(pairs_dev, dtype=jnp.int32)
    position = (pair_index - own_start)[:, None] * per_frame + jnp.arange(
        per_frame, dtype=jnp.int32
    )[None, :]
    live = (position < own_keep[:, None]).reshape(-1).astype(jnp.bfloat16)
    pre = lax.psum(contract_last(patches, sampler_rows), "tp")
    act = jax.nn.silu(pre).astype(jnp.bfloat16)
    tokens = (
        jnp.dot(act, full_readout, preferred_element_type=jnp.float32).astype(jnp.bfloat16)
        * live[:, None]
    )
    llm_tokens = lax.all_to_all(tokens, "ctx", split_axis=0, concat_axis=0, tiled=True)
    back = (
        lax.all_to_all(token_cotangent, "ctx", split_axis=0, concat_axis=0, tiled=True)
        * live[:, None]
    )
    grad_act = lax.psum(contract_last(back, full_readout), "tp")
    grad_pre = (grad_act * silu_slope(pre)).astype(jnp.bfloat16)
    grad_patches = jnp.dot(grad_pre, sampler_rows, preferred_element_type=jnp.float32)
    grad_taps = unpatch(grad_patches, pairs_dev, SIDE, chans)
    leading = grad_taps[:, 0] * pair_mask[:, None, None, None]
    incoming = shifted(leading[0].astype(jnp.bfloat16), "ctx", -1).astype(jnp.float32)
    grad_even = grad_taps[:, 1]
    grad_odd = jnp.concatenate([leading[1:], incoming[None]], axis=0)
    grad_hidden = jnp.stack([grad_even, grad_odd], axis=1).reshape(frames_dev, SIDE, SIDE, chans)
    grad_excite = jnp.sum(grad_hidden * active, axis=(1, 2))
    grad_inner = grad_excite * excite * (1.0 - excite)
    grad_relaxed = lax.psum(
        jnp.dot(grad_inner, squeeze_out.astype(jnp.float32).T, precision=highest), "tp"
    )
    grad_squeezed = grad_relaxed * silu_slope(squeezed)
    grad_pooled = jnp.dot(grad_squeezed, squeeze_in.astype(jnp.float32).T, precision=highest)
    grad_active = grad_hidden * excite[:, None, None, :] + grad_pooled[:, None, None, :] / cells
    grad_conv = (grad_active * silu_slope(conv_out)).astype(jnp.bfloat16)
    grad_grid = grad_hidden + grouped_backward(grad_conv, group_kernel)
    grad_features = grad_grid.astype(jnp.bfloat16).reshape(frames_dev, cells, chans)
    return (llm_tokens, grad_features)


def solution(mesh):
    placed = (
        P("ctx", None, "tp"),
        P(None, "tp", None),
        P("tp", None),
        P(None, "tp"),
        P("ctx", None, "tp"),
        P("ctx", "tp"),
        P(),
        P(),
        P("ctx", "tp"),
    )
    return jax.shard_map(
        per_device,
        mesh=mesh,
        in_specs=placed,
        out_specs=(P("ctx", "tp"), P("ctx", None, "tp")),
        check_vma=False,
    )
```

profile of v0, /device:TPU:6, one launch (start us, length us, event | category | flops | bytes accessed | tf_op | source)
XLA Modules:
  0.0 348.0 jit_solution(8308310035529797624)
XLA Ops:
  7.2 0.7 all-gather.6.cloned.1.call-update
  8.0 0.7 all-gather.4.cloned.1.call-update
  8.7 1.1 copy.230
  9.7 1.0 copy.240
  10.8 1.5 fusion.52
  12.4 2.3 pad_slice_fusion
  17.0 1.2 reshape.191
  18.2 0.8 copy.246
  19.0 2.0 reshape.192
  21.2 2.0 reshape.193
  26.3 0.6 reshape.194
  27.1 17.6 %psum.28 = f32[2,288]{1,0:T(2,128)S(1)} all-reduce(f32[2,288]{1,0:T(2,128)S(1)} %fusion.54), channel_id=1, replica_groups=mesh['ctx'=64,'tp'=8] {'tp'}, use_global_device_ids=true, to_apply=%region_1.2 | all-reduce | flops 576 | bytes 4608 | tf_op jit(solution)/shard_map/psum | solution.py:98
  44.7 0.6 copy-done.28
  45.6 1.4 add_convert_fusion
  47.2 1.9 collective-permute-start
  49.1 0.5 broadcast.98
  49.7 0.7 reduce.6
  50.3 0.7 reshape.225
  51.1 15.2 %all-to-all-start.1 = ((bf16[64,2,512]{2,1,0:T(2,128)(2,1)}), bf16[64,2,512]{2,1,0:T(2,128)(2,1)S(1)}, u32[]{:S(2)}, u32[]{:S(2)}) async-start(bf16[64,2,512]{2,1,0:T(2,128)(2,1)} %reshape.225), calls=%async_computation.1 | async-start | bytes 262144 | tf_op jit(solution)/shard_map/all_to_all | solution.py:141
  66.8 0.6 dynamic_slice.6
  68.1 0.7 fusion.45
  69.5 0.7 fusion.46
  70.1 0.7 compare_convert_fusion
  71.6 0.9 reshape.196
  72.5 2.6 all-to-all-done.1
  75.3 24.2 %all-gather.6.cloned.1.call-done = bf16[64,18,1024]{2,1,0:T(8,128)(2,1)} async-done(((bf16[1,18,1024]{2,1,0:T(8,128)(2,1)}), bf16[64,18,1024]{2,1,0:T(8,128)(2,1)}) %all-gather.6.cloned.1.call-update) | async-done | bytes 2359312 | tf_op jit(solution)/shard_map/all_gather | solution.py:104
  99.5 2.9 reshape.212
  102.4 1.6 fusion.29
  104.0 81.3 %all-gather.4.cloned.1.call-done = bf16[1152,8,144]{2,1,0:T(8,128)(2,1)} async-done(((bf16[18,8,144]{2,1,0:T(8,128)(2,1)}), bf16[1152,8,144]{2,1,0:T(8,128)(2,1)}) %all-gather.4.cloned.1.call-update) | async-done | bytes 2654224 | tf_op jit(solution)/shard_map/all_gather | solution.py:103
  185.3 5.5 %copy.254 = bf16[1152,8,144]{0,2,1:T(8,128)(2,1)S(1)} copy(bf16[1152,8,144]{2,1,0:T(8,128)(2,1)} %all-gather.4.cloned.1.call-done) | data formatting | bytes 5308416 | tf_op jit(solution)/shard_map/all_gather | solution.py:103
  190.8 2.2 fusion.55
  193.1 77.1 %all-reduce.14.cloned.1.call-done = (f32[64,1152]{1,0:T(8,128)}, f32[64,1152]{1,0:T(8,128)}) async-done(((f32[64,1152]{1,0:T(8,128)}, f32[64,1152]{1,0:T(8,128)}), (f32[64,1152]{1,0:T(8,128)}, f32[64,1152]{1,0:T(8,128)})) %all-reduce.14.cloned.1.call-update) | async-done | bytes 589840 | tf_op jit(solution)/shard_map/psum | solution.py:144
  270.3 2.3 convolution_bitcast_fusion.14
  273.0 0.8 fusion.51
  273.8 2.1 collective-permute-start.1
  275.9 0.5 fusion.7
  276.7 0.7 reduce.7
  277.4 0.7 reshape.227
  278.1 11.2 %all-to-all-start = ((bf16[64,2,512]{2,1,0:T(2,128)(2,1)}), bf16[64,2,512]{2,1,0:T(2,128)(2,1)S(1)}, u32[]{:S(2)}, u32[]{:S(2)}) async-start(bf16[64,2,512]{2,1,0:T(2,128)(2,1)} %reshape.227), calls=%async_computation | async-start | bytes 262144 | tf_op jit(solution)/shard_map/all_to_all | solution.py:139
  289.5 0.5 multiply_reduce_fusion.1
  290.1 16.7 %psum.31 = f32[2,288]{1,0:T(2,128)S(1)} all-reduce(f32[2,288]{1,0:T(2,128)S(1)} %fusion.39), channel_id=1, replica_groups=mesh['ctx'=64,'tp'=8] {'tp'}, use_global_device_ids=true, to_apply=%region_8.9 | all-reduce | flops 576 | bytes 4608 | tf_op jit(solution)/shard_map/psum | solution.py:155
  308.1 1.1 convolution_bitcast_fusion.7
  309.2 1.1 convolution_bitcast_fusion.6
  310.3 1.1 convolution_bitcast_fusion.5
  311.4 1.1 convolution_bitcast_fusion.4
  312.6 1.1 convolution_bitcast_fusion.3
  314.8 1.3 reshape.201
  316.2 1.5 copy.264
  317.7 1.4 reshape.202
  319.0 1.5 copy.265
  320.5 1.4 reshape.203
  321.9 1.5 copy.266
  323.4 1.4 reshape.204
  324.8 1.5 copy.267
  326.3 1.4 reshape.205
  327.7 1.5 copy.268
  329.2 1.3 reshape.206
  330.9 1.4 reshape.207
  332.7 1.4 reshape.208
  334.5 1.4 reshape.209
  335.9 1.5 pad_add_fusion
  337.4 2.4 fusion.15
  339.8 0.8 copy.272
  340.7 0.7 copy.321
  (140 shorter events, 12.3 us)
Async XLA Ops:
  7.2 38.1 %copy-start = (bf16[288,144]{0,1:T(8,128)(2,1)S(1)}, bf16[288,144]{0,1:T(8,128)(2,1)}, u32[]{:S(2)}) copy-start(bf16[288,144]{0,1:T(8,128)(2,1)} %param.12) | copy-start | bytes 248836
  7.2 92.3 %all-gather.6.cloned.1.call-start = ((), (), s32[]{:S(2)}) async-start(), calls=%async_computation.3 | async-start | bytes 3194880 | tf_op jit(solution)/shard_map/all_gather | solution.py:104
  7.9 177.4 %all-gather.4.cloned.1.call-start = ((), (), s32[]{:S(2)}) async-start(), calls=%async_computation.2 | async-start | bytes 4792320 | tf_op jit(solution)/shard_map/all_gather | solution.py:103
  15.1 8.3 %copy-start.9 = (bf16[1,144,48]{2,1,0:T(8,128)(2,1)}, bf16[1,144,48]{2,1,0:T(8,128)(2,1)S(1)}, u32[]{:S(2)}) copy-start(bf16[1,144,48]{2,1,0:T(8,128)(2,1)S(1)} %copy.233) | copy-start | bytes 41476
  15.5 8.2 %copy-start.11 = (bf16[1,144,48]{2,1,0:T(8,128)(2,1)}, bf16[1,144,48]{2,1,0:T(8,128)(2,1)S(1)}, u32[]{:S(2)}) copy-start(bf16[1,144,48]{2,1,0:T(8,128)(2,1)S(1)} %copy.235) | copy-start | bytes 41476
  15.8 8.0 %copy-start.13 = (bf16[1,144,48]{2,1,0:T(8,128)(2,1)}, bf16[1,144,48]{2,1,0:T(8,128)(2,1)S(1)}, u32[]{:S(2)}) copy-start(bf16[1,144,48]{2,1,0:T(8,128)(2,1)S(1)} %copy.237) | copy-start | bytes 41476
  16.2 7.9 %copy-start.15 = (bf16[1,144,48]{2,1,0:T(8,128)(2,1)}, bf16[1,144,48]{2,1,0:T(8,128)(2,1)S(1)}, u32[]{:S(2)}) copy-start(bf16[1,144,48]{2,1,0:T(8,128)(2,1)S(1)} %copy.239) | copy-start | bytes 41476
  16.6 7.8 %copy-start.17 = (bf16[1,144,48]{2,1,0:T(8,128)(2,1)}, bf16[1,144,48]{2,1,0:T(8,128)(2,1)S(1)}, u32[]{:S(2)}) copy-start(bf16[1,144,48]{2,1,0:T(8,128)(2,1)S(1)} %copy.242) | copy-start | bytes 41476
  16.9 7.7 %copy-start.19 = (bf16[1,144,48]{2,1,0:T(8,128)(2,1)}, bf16[1,144,48]{2,1,0:T(8,128)(2,1)S(1)}, u32[]{:S(2)}) copy-start(bf16[1,144,48]{2,1,0:T(8,128)(2,1)S(1)} %copy.244) | copy-start | bytes 41476
  19.0 5.9 %copy-start.21 = (bf16[1,144,48]{2,1,0:T(8,128)(2,1)}, bf16[1,144,48]{2,1,0:T(8,128)(2,1)S(1)}, u32[]{:S(2)}) copy-start(bf16[1,144,48]{2,1,0:T(8,128)(2,1)S(1)} %copy.246) | copy-start | bytes 41476
  21.2 4.2 %copy-start.23 = (bf16[1,144,48]{2,1,0:T(8,128)(2,1)}, bf16[1,144,48]{2,1,0:T(8,128)(2,1)S(1)}, u32[]{:S(2)}) copy-start(bf16[1,144,48]{2,1,0:T(8,128)(2,1)S(1)} %copy.248) | copy-start | bytes 41476
  24.1 1.0 copy-start.7
  24.4 1.0 copy-start.8
  25.4 1.5 copy-start.26
  25.8 23.9 %copy-start.25 = (bf16[64,1024]{1,0:T(8,128)(2,1)S(1)}, bf16[64,1024]{1,0:T(8,128)(2,1)}, u32[]{:S(2)}) copy-start(bf16[64,1024]{1,0:T(8,128)(2,1)} %param.17) | copy-start | bytes 393220
  26.3 40.2 %copy-start.33 = (s32[128]{0:T(128)S(1)}, s32[128]{0:T(128)}, u32[]{:S(2)}) copy-start(s32[128]{0:T(128)} %param.15) | copy-start | bytes 1540
  26.3 43.2 %copy-start.34 = (s32[16]{0:T(128)S(1)}, s32[16]{0:T(128)}, u32[]{:S(2)}) copy-start(s32[16]{0:T(128)} %param.16) | copy-start | bytes 196
  44.7 0.6 copy-start.28
  47.2 23.6 %collective-permute-start = (bf16[14,14,144]{2,1,0:T(8,128)(2,1)S(1)}, bf16[14,14,144]{2,1,0:T(8,128)(2,1)S(1)}, u32[]{:S(2)}, u32[]{:S(2)}) collective-permute-start(bf16[14,14,144]{2,1,0:T(8,128)(2,1)S(1)} %bitcast.239), channel_id=1, source_target_pairs={{0,8},{8,16},{16,24},{24,32},{32,40},{40,48},{48,56},{56,64},{64,7... | collective-permute-start | bytes 169352 | tf_op jit(solution)/shard_map/ppermute | solution.py:13
  51.1 24.1 %all-to-all-start.1 = ((bf16[64,2,512]{2,1,0:T(2,128)(2,1)}), bf16[64,2,512]{2,1,0:T(2,128)(2,1)S(1)}, u32[]{:S(2)}, u32[]{:S(2)}) async-start(bf16[64,2,512]{2,1,0:T(2,128)(2,1)} %reshape.225), calls=%async_computation.1 | async-start | bytes 262144 | tf_op jit(solution)/shard_map/all_to_all | solution.py:141
  66.3 204.0 %all-reduce.14.cloned.1.call-start = ((), (), s32[]{:S(2)}) async-start(), calls=%async_computation.4 | async-start | bytes 1179648 | tf_op jit(solution)/shard_map/psum | solution.py:144
  70.8 31.6 %copy-start.30 = (bf16[64]{0:T(256)(128)(2,1)}, bf16[64]{0:T(256)(128)(2,1)S(1)}, u32[]{:S(2)}) copy-start(bf16[64]{0:T(256)(128)(2,1)S(1)} %compare_convert_fusion) | copy-start | bytes 388
  102.4 1.6 copy-start.1
  270.3 5.6 %copy-start.2 = (bf16[1152,1024]{1,0:T(8,128)(2,1)S(1)}, bf16[1152,1024]{1,0:T(8,128)(2,1)}, u32[]{:S(2)}) copy-start(bf16[1152,1024]{1,0:T(8,128)(2,1)} %copy-done.1) | copy-start | bytes 7077892
  270.3 5.6 %copy-start.31 = (bf16[64]{0:T(256)(128)(2,1)S(1)}, bf16[64]{0:T(256)(128)(2,1)}, u32[]{:S(2)}) copy-start(bf16[64]{0:T(256)(128)(2,1)} %copy-done.30) | copy-start | bytes 388
  270.3 5.6 %copy-start.32 = (f32[64,1152]{1,0:T(8,128)S(1)}, f32[64,1152]{1,0:T(8,128)}, u32[]{:S(2)}) copy-start(f32[64,1152]{1,0:T(8,128)} %get-tuple-element.15) | copy-start | bytes 884740
  273.8 15.7 %copy-start.3 = (f32[2,14,14,144]{3,0,2,1:T(2,128)S(1)}, f32[2,14,14,144]{3,0,2,1:T(2,128)}, u32[]{:S(2)}) copy-start(f32[2,14,14,144]{3,0,2,1:T(2,128)} %get-tuple-element.17) | copy-start | bytes 677380
  273.8 33.1 %copy-start.27 = (bf16[144,288]{1,0:T(8,128)(2,1)S(1)}, bf16[144,288]{1,0:T(8,128)(2,1)}, u32[]{:S(2)}) copy-start(bf16[144,288]{1,0:T(8,128)(2,1)} %param.11) | copy-start | bytes 248836
  273.8 33.1 %copy-start.29 = (f32[2,288]{1,0:T(2,128)S(1)}, f32[2,288]{1,0:T(2,128)}, u32[]{:S(2)}) copy-start(f32[2,288]{1,0:T(2,128)} %copy-done.28) | copy-start | bytes 6916
  273.8 15.5 %collective-permute-start.1 = (bf16[14,14,144]{2,1,0:T(8,128)(2,1)S(1)}, bf16[14,14,144]{2,1,0:T(8,128)(2,1)S(1)}, u32[]{:S(2)}, u32[]{:S(2)}) collective-permute-start(bf16[14,14,144]{2,1,0:T(8,128)(2,1)S(1)} %fusion.31), channel_id=1, source_target_pairs={{8,0},{16,8},{24,16},{32,24},{40,32},{48,40},{56,48},{64,56},{72,6... | collective-permute-start | bytes 169352 | tf_op jit(solution)/shard_map/ppermute | solution.py:13
  278.1 62.5 %all-to-all-start = ((bf16[64,2,512]{2,1,0:T(2,128)(2,1)}), bf16[64,2,512]{2,1,0:T(2,128)(2,1)S(1)}, u32[]{:S(2)}, u32[]{:S(2)}) async-start(bf16[64,2,512]{2,1,0:T(2,128)(2,1)} %reshape.227), calls=%async_computation | async-start | bytes 262144 | tf_op jit(solution)/shard_map/all_to_all | solution.py:139
  289.3 18.8 %copy-start.10 = (bf16[1,144,48]{2,1,0:T(8,128)(2,1)S(1)}, bf16[1,144,48]{2,1,0:T(8,128)(2,1)}, u32[]{:S(2)}) copy-start(bf16[1,144,48]{2,1,0:T(8,128)(2,1)} %copy-done.9) | copy-start | bytes 41476
  290.1 19.1 %copy-start.12 = (bf16[1,144,48]{2,1,0:T(8,128)(2,1)S(1)}, bf16[1,144,48]{2,1,0:T(8,128)(2,1)}, u32[]{:S(2)}) copy-start(bf16[1,144,48]{2,1,0:T(8,128)(2,1)} %copy-done.11) | copy-start | bytes 41476
  307.5 2.9 copy-start.14
  307.5 3.9 %copy-start.16 = (bf16[1,144,48]{2,1,0:T(8,128)(2,1)S(1)}, bf16[1,144,48]{2,1,0:T(8,128)(2,1)}, u32[]{:S(2)}) copy-start(bf16[1,144,48]{2,1,0:T(8,128)(2,1)} %copy-done.15) | copy-start | bytes 41476
  307.9 4.7 %copy-start.18 = (bf16[1,144,48]{2,1,0:T(8,128)(2,1)S(1)}, bf16[1,144,48]{2,1,0:T(8,128)(2,1)}, u32[]{:S(2)}) copy-start(bf16[1,144,48]{2,1,0:T(8,128)(2,1)} %copy-done.17) | copy-start | bytes 41476
  308.1 5.5 %copy-start.20 = (bf16[1,144,48]{2,1,0:T(8,128)(2,1)S(1)}, bf16[1,144,48]{2,1,0:T(8,128)(2,1)}, u32[]{:S(2)}) copy-start(bf16[1,144,48]{2,1,0:T(8,128)(2,1)} %copy-done.19) | copy-start | bytes 41476
  309.2 4.7 %copy-start.22 = (bf16[1,144,48]{2,1,0:T(8,128)(2,1)S(1)}, bf16[1,144,48]{2,1,0:T(8,128)(2,1)}, u32[]{:S(2)}) copy-start(bf16[1,144,48]{2,1,0:T(8,128)(2,1)} %copy-done.21) | copy-start | bytes 41476
  310.3 3.8 %copy-start.24 = (bf16[1,144,48]{2,1,0:T(8,128)(2,1)S(1)}, bf16[1,144,48]{2,1,0:T(8,128)(2,1)}, u32[]{:S(2)}) copy-start(bf16[1,144,48]{2,1,0:T(8,128)(2,1)} %copy-done.23) | copy-start | bytes 41476
  332.3 3.6 %copy-start.4 = (f32[2,14,14,144]{3,0,2,1:T(2,128)S(1)}, f32[2,14,14,144]{3,0,2,1:T(2,128)}, u32[]{:S(2)}) copy-start(f32[2,14,14,144]{3,0,2,1:T(2,128)} %reshape.201) | copy-start | bytes 677380
  334.1 3.3 copy-start.5
  334.5 2.9 copy-start.6
Sparse Core Ops, SparseCore 0:
  11.3 88.0 all-gather.5
  102.8 82.4 all-gather.3
  193.2 77.0 all-reduce.13
where the time goes:
time: 349 us; the launch traced here: 348 us
  waiting for transfers between devices  187 us (54%)
  local copies, waits for them, and re-layouts  54.8 us (16%)
  blocking collectives  34.3 us (10%)
  starting transfers between devices  30.7 us (9%)
  matrix products  16 us (5%)
  between operations  15.9 us (5%)
  other arithmetic  9.59 us (3%)
    all_gather x1, waiting for transfers between devices, per_device(): lax.all_gather(sampler_kernel, 'ctx', axis=0, tiled=True)  81.3 us
    psum x1, waiting for transfers between devices, per_device(): grad_act = lax.psum(contract_last(back, full_readout), 'tp')  77.1 us
    all_gather x1, waiting for transfers between devices, per_device(): lax.all_gather(readout_kernel, 'ctx', axis=0, tiled=True)  24.2 us
    psum x1, blocking collectives, per_device(): lax.psum(jnp.dot(pooled, squeeze_in.astype(jnp.float32), precision=highes...  17.6 us
    psum x1, blocking collectives, per_device(): lax.psum(jnp.dot(grad_inner, squeeze_out.astype(jnp.float32).T, precision...  16.7 us
    all_to_all x1, starting transfers between devices, per_device(): lax.all_to_all(token_cotangent, 'ctx', split_axis=0, concat_axis=0, tiled...  15.2 us
    reshape x9, local copies, waits for them, and re-layouts, grouped_backward(): spread = spread.reshape(count, side, side, chans)  12.2 us
    all_to_all x1, starting transfers between devices, per_device(): lax.all_to_all(tokens, 'ctx', split_axis=0, concat_axis=0, tiled=True)  11.2 us
  transfers between devices with their start and end apart: 7, of which 4 were waited for; matrix products, arithmetic and copies ran while one was open for 19% of the time, Pallas kernels for 0%

commit v1 on v0

--- a/solution.py
+++ b/solution.py
@@ -101,7 +101,9 @@
     hidden = (grid.astype(jnp.float32) + active * excite[:, None, None, :]).astype(jnp.bfloat16)
     full_sampler, full_readout = (
         lax.all_gather(sampler_kernel, "ctx", axis=0, tiled=True),
-        lax.all_gather(readout_kernel, "ctx", axis=0, tiled=True),
+        jnp.concatenate(
+            lax.all_to_all(jnp.stack([readout_kernel] * lax.axis_size("ctx")), "ctx", 0, 0), axis=0
+        ),
     )
     sampler_rows = full_sampler.reshape(full_sampler.shape[0], 8 * chans)
     halo_frame = shifted(hidden[-1], "ctx", 1)

time: 349 us -> 303 us (0.87)
  waiting for transfers between devices: 187 us -> 96.3 us
  local copies, waits for them, and re-layouts: 54.8 us -> 83.6 us
  starting transfers between devices: 30.7 us -> 35.8 us
  matrix products: 16 us -> 20.7 us
  other arithmetic: 9.59 us -> 13.9 us
    all_gather x1, waiting for transfers between devices: 81.3 us -> 0.01 us  [per_device(): lax.all_gather(sampler_kernel, 'ctx', axis=0, tiled=True)]
    all_gather x1 -> x0, waiting for transfers between devices: 24.2 us -> none  [per_device(): lax.all_gather(readout_kernel, 'ctx', axis=0, tiled=True)]
    ppermute x2, waiting for transfers between devices: 0.01 us -> 13 us  [shifted(): return lax.ppermute(value, axis, pairs)]
    reshape x9, local copies, waits for them, and re-layouts: 6.7 us -> 17.6 us  [grouped_forward(): window = window.reshape(count, side, side, groups, width)]
    slice x10, local copies, waits for them, and re-layouts: 3.24 us -> 11.9 us  [grouped_forward(): kernel[kernel_tap]]
    all_to_all x0 -> x1, starting transfers between devices: none -> 6.37 us  [per_device(): lax.all_to_all(jnp.stack([readout_kernel] * lax.axis_size('ctx')), 'ctx',...]
    unnamed x82 -> x93, local copies, waits for them, and re-layouts: 9.5 us -> 9.39 us
  transfers between devices with their start and end apart: 7 -> 7, of which waited for: 4 -> 3; matrix products, arithmetic and copies ran while one was open for 19% -> 35% of each run, Pallas kernels for 0% -> 0%
where the time goes in v1:
time: 303 us; the launch traced here: 301 us
  waiting for transfers between devices  96.3 us (32%)
  local copies, waits for them, and re-layouts  83.6 us (28%)
  starting transfers between devices  35.8 us (12%)
  blocking collectives  34.3 us (11%)
  matrix products  20.7 us (7%)
  between operations  16.2 us (5%)
  other arithmetic  13.9 us (5%)
    psum x1, waiting for transfers between devices, per_device(): grad_act = lax.psum(contract_last(back, full_readout), 'tp')  78.2 us
    reshape x9, local copies, waits for them, and re-layouts, grouped_forward(): window = window.reshape(count, side, side, groups, width)  17.6 us
    psum x1, blocking collectives, per_device(): lax.psum(jnp.dot(pooled, squeeze_in.astype(jnp.float32), precision=highes...  17.5 us
    psum x1, blocking collectives, per_device(): lax.psum(jnp.dot(grad_inner, squeeze_out.astype(jnp.float32).T, precision...  16.8 us
    all_to_all x1, starting transfers between devices, per_device(): lax.all_to_all(token_cotangent, 'ctx', split_axis=0, concat_axis=0, tiled...  14 us
    ppermute x2, waiting for transfers between devices, shifted(): return lax.ppermute(value, axis, pairs)  13 us
    reshape x9, local copies, waits for them, and re-layouts, grouped_backward(): spread = spread.reshape(count, side, side, chans)  12.2 us
    slice x10, local copies, waits for them, and re-layouts, grouped_forward(): kernel[kernel_tap]  11.9 us
  transfers between devices with their start and end apart: 7, of which 3 were waited for; matrix products, arithmetic and copies ran while one was open for 35% of the time, Pallas kernels for 0%

profile of v1, /device:TPU:6, one launch (start us, length us, event | category | flops | bytes accessed | tf_op | source)
XLA Modules:
  0.0 300.8 jit_solution(7824005747777606082)
XLA Ops:
  8.4 1.6 reduce.6
  10.7 14.0 %all-to-all-start.2 = ((bf16[64,2,512]{2,1,0:T(2,128)(2,1)}), bf16[64,2,512]{2,1,0:T(2,128)(2,1)S(1)}, u32[]{:S(2)}, u32[]{:S(2)}) async-start(bf16[64,2,512]{2,1,0:T(2,128)(2,1)} %reshape.236), calls=%async_computation.2 | async-start | bytes 262144 | tf_op jit(solution)/shard_map/all_to_all | solution.py:143
  25.8 1.7 copy.241
  27.6 1.5 fusion.52
  29.2 4.4 %all-to-all-done.2 = bf16[64,2,512]{2,1,0:T(2,128)(2,1)S(1)} async-done(((bf16[64,2,512]{2,1,0:T(2,128)(2,1)}), bf16[64,2,512]{2,1,0:T(2,128)(2,1)S(1)}, u32[]{:S(2)}, u32[]{:S(2)}) %all-to-all-start.2) | async-done | bytes 131104 | tf_op jit(solution)/shard_map/all_to_all | solution.py:143
  33.6 2.9 stack.19
  36.5 6.4 %all-to-all-start = ((bf16[64,18,1024]{2,1,0:T(8,128)(2,1)}), bf16[64,18,1024]{2,1,0:T(8,128)(2,1)S(1)}, u32[]{:S(2)}, u32[]{:S(2)}) async-start(bf16[64,18,1024]{2,1,0:T(8,128)(2,1)} %stack.19), calls=%async_computation | async-start | bytes 6291456 | tf_op jit(solution)/shard_map/all_to_all | solution.py:105
  42.9 2.5 pad_slice_fusion
  45.4 2.0 reshape.197
  48.3 2.0 reshape.198
  50.3 1.4 copy.236
  51.7 2.0 reshape.199
  53.7 1.5 copy.238
  55.2 1.9 reshape.200
  57.1 1.4 copy.240
  58.5 1.9 reshape.201
  60.5 1.5 copy.243
  61.9 2.0 reshape.202
  63.9 1.5 copy.245
  65.3 2.0 reshape.203
  67.3 1.4 copy.247
  68.7 1.9 reshape.204
  71.4 1.9 reshape.205
  73.4 1.4 fusion.24
  74.8 1.3 convolution_add_fusion.2
  78.0 1.2 multiply_reduce_fusion
  79.4 2.5 copy.251
  81.8 2.5 reshape.206
  85.4 17.5 %psum.28 = f32[2,288]{1,0:T(2,128)S(1)} all-reduce(f32[2,288]{1,0:T(2,128)S(1)} %fusion.54), channel_id=1, replica_groups=mesh['ctx'=64,'tp'=8] {'tp'}, use_global_device_ids=true, to_apply=%region_1.2 | all-reduce | flops 576 | bytes 4608 | tf_op jit(solution)/shard_map/psum | solution.py:98
  103.2 2.3 add_convert_fusion
  106.5 2.1 collective-permute-start
  113.1 1.2 compare_convert_fusion
  114.3 13.0 %collective-permute-done = bf16[14,14,144]{2,1,0:T(8,128)(2,1)} collective-permute-done((bf16[14,14,144]{2,1,0:T(8,128)(2,1)}, bf16[14,14,144]{2,1,0:T(8,128)(2,1)}, u32[]{:S(2)}, u32[]{:S(2)}) %collective-permute-start) | collective-permute-done | bytes 56480 | tf_op jit(solution)/shard_map/ppermute | solution.py:13
  130.7 1.4 reshape.237
  132.1 2.3 reshape.210
  134.4 3.2 %fusion.29 = f32[64,1152]{1,0:T(8,128)} fusion(bf16[1152,1024]{1,0:T(8,128)(2,1)} %reshape.210, bf16[64,1,1024]{2,1,0:T(2,128)(2,1)S(1)} %reshape.237, bf16[64]{0:T(256)(128)(2,1)} %compare_convert_fusion), kind=kOutput, calls=%fused_computation.70 | convolution fusion | flops 151060480 | bytes 2785408 | tf_op jit(solution)/shard_map/dot_general | solution.py:74
  137.6 5.5 %copy.255 = bf16[1152,8,144]{0,2,1:T(8,128)(2,1)S(1)} copy(bf16[1152,8,144]{2,1,0:T(8,128)(2,1)} %all-gather.2.cloned.1.call-done) | data formatting | bytes 5308416 | tf_op jit(solution)/shard_map/all_gather | solution.py:103
  143.2 1.3 fusion.55
  144.7 78.2 %all-reduce.14.cloned.1.call-done = (f32[64,1152]{1,0:T(8,128)}, f32[64,1152]{1,0:T(8,128)}) async-done(((f32[64,1152]{1,0:T(8,128)}, f32[64,1152]{1,0:T(8,128)}), (f32[64,1152]{1,0:T(8,128)}, f32[64,1152]{1,0:T(8,128)})) %all-reduce.14.cloned.1.call-update) | async-done | bytes 589840 | tf_op jit(solution)/shard_map/psum | solution.py:146
  222.9 2.3 convolution_bitcast_fusion.14
  226.4 2.1 collective-permute-start.1
  230.7 11.2 %all-to-all-start.1 = ((bf16[64,2,512]{2,1,0:T(2,128)(2,1)}), bf16[64,2,512]{2,1,0:T(2,128)(2,1)S(1)}, u32[]{:S(2)}, u32[]{:S(2)}) async-start(bf16[64,2,512]{2,1,0:T(2,128)(2,1)} %reshape.238), calls=%async_computation.1 | async-start | bytes 262144 | tf_op jit(solution)/shard_map/all_to_all | solution.py:141
  242.7 16.8 %psum.31 = f32[2,288]{1,0:T(2,128)S(1)} all-reduce(f32[2,288]{1,0:T(2,128)S(1)} %fusion.39), channel_id=1, replica_groups=mesh['ctx'=64,'tp'=8] {'tp'}, use_global_device_ids=true, to_apply=%region_8.9 | all-reduce | flops 576 | bytes 4608 | tf_op jit(solution)/shard_map/psum | solution.py:157
  260.8 1.1 convolution_bitcast_fusion.7
  261.9 1.1 convolution_bitcast_fusion.6
  263.0 1.1 convolution_bitcast_fusion.5
  264.0 1.1 convolution_bitcast_fusion.4
  265.2 1.1 convolution_bitcast_fusion.3
  267.4 1.4 reshape.214
  268.8 1.5 copy.266
  270.3 1.3 reshape.215
  271.6 1.5 copy.267
  273.1 1.3 reshape.216
  274.5 1.5 copy.268
  276.0 1.4 reshape.217
  277.4 1.5 copy.269
  278.9 1.4 reshape.218
  280.2 1.5 copy.270
  281.8 1.3 reshape.219
  283.5 1.4 reshape.220
  285.3 1.4 reshape.221
  287.1 1.4 reshape.222
  288.4 1.4 pad_add_fusion
  289.9 2.5 fusion.15
  (152 shorter events, 24.9 us)
Async XLA Ops:
  7.2 95.8 %copy-start = (bf16[288,144]{0,1:T(8,128)(2,1)S(1)}, bf16[288,144]{0,1:T(8,128)(2,1)}, u32[]{:S(2)}) copy-start(bf16[288,144]{0,1:T(8,128)(2,1)} %param.12) | copy-start | bytes 248836
  7.2 130.5 %all-gather.2.cloned.1.call-start = ((), (), s32[]{:S(2)}) async-start(), calls=%async_computation.3 | async-start | bytes 4792320 | tf_op jit(solution)/shard_map/all_gather | solution.py:103
  10.7 22.9 %all-to-all-start.2 = ((bf16[64,2,512]{2,1,0:T(2,128)(2,1)}), bf16[64,2,512]{2,1,0:T(2,128)(2,1)S(1)}, u32[]{:S(2)}, u32[]{:S(2)}) async-start(bf16[64,2,512]{2,1,0:T(2,128)(2,1)} %reshape.236), calls=%async_computation.2 | async-start | bytes 262144 | tf_op jit(solution)/shard_map/all_to_all | solution.py:143
  33.6 2.9 copy-start.14
  36.5 95.6 %all-to-all-start = ((bf16[64,18,1024]{2,1,0:T(8,128)(2,1)}), bf16[64,18,1024]{2,1,0:T(8,128)(2,1)S(1)}, u32[]{:S(2)}, u32[]{:S(2)}) async-start(bf16[64,18,1024]{2,1,0:T(8,128)(2,1)} %stack.19), calls=%async_computation | async-start | bytes 6291456 | tf_op jit(solution)/shard_map/all_to_all | solution.py:105
  42.9 180.0 %all-reduce.14.cloned.1.call-start = ((), (), s32[]{:S(2)}) async-start(), calls=%async_computation.4 | async-start | bytes 1179648 | tf_op jit(solution)/shard_map/psum | solution.py:146
  48.3 26.5 %copy-start.16 = (bf16[1,144,48]{2,1,0:T(8,128)(2,1)}, bf16[1,144,48]{2,1,0:T(8,128)(2,1)S(1)}, u32[]{:S(2)}) copy-start(bf16[1,144,48]{2,1,0:T(8,128)(2,1)S(1)} %copy.234) | copy-start | bytes 41476
  73.3 2.8 copy-start.7
  73.3 2.8 copy-start.18
  73.4 3.0 %copy-start.8 = (bf16[2,14,14,3,48]{4,3,0,2,1:T(4,128)(2,1)S(1)}, bf16[2,14,14,3,48]{4,3,0,2,1:T(4,128)(2,1)}, u32[]{:S(2)}) copy-start(bf16[2,14,14,3,48]{4,3,0,2,1:T(4,128)(2,1)} %reshape.200) | copy-start | bytes 338692
  73.4 3.1 %copy-start.20 = (bf16[1,144,48]{2,1,0:T(8,128)(2,1)S(1)}, bf16[1,144,48]{2,1,0:T(8,128)(2,1)}, u32[]{:S(2)}) copy-start(bf16[1,144,48]{2,1,0:T(8,128)(2,1)} %copy.238) | copy-start | bytes 41476
  74.8 1.9 copy-start.9
  74.8 1.9 copy-start.22
  76.1 1.0 copy-start.10
  76.1 1.0 copy-start.24
  76.4 1.0 copy-start.11
  76.4 1.0 copy-start.26
  76.7 1.1 copy-start.12
  76.7 1.1 copy-start.28
  76.9 1.1 copy-start.15
  76.9 1.1 copy-start.30
  79.3 29.2 %copy-start.39 = (s32[128]{0:T(128)S(1)}, s32[128]{0:T(128)}, u32[]{:S(2)}) copy-start(s32[128]{0:T(128)} %param.15) | copy-start | bytes 1540
  79.4 33.0 %copy-start.40 = (s32[16]{0:T(128)S(1)}, s32[16]{0:T(128)}, u32[]{:S(2)}) copy-start(s32[16]{0:T(128)} %param.16) | copy-start | bytes 196
  102.9 26.7 %copy-start.35 = (f32[2,288]{1,0:T(2,128)}, f32[2,288]{1,0:T(2,128)S(1)}, u32[]{:S(2)}) copy-start(f32[2,288]{1,0:T(2,128)S(1)} %psum.28) | copy-start | bytes 6916
  103.2 26.4 %copy-start.33 = (f32[2,144]{1,0:T(2,128)}, f32[2,144]{1,0:T(2,128)S(1)}, u32[]{:S(2)}) copy-start(f32[2,144]{1,0:T(2,128)S(1)} %fusion.10) | copy-start | bytes 3460
  106.5 20.8 %collective-permute-start = (bf16[14,14,144]{2,1,0:T(8,128)(2,1)}, bf16[14,14,144]{2,1,0:T(8,128)(2,1)}, u32[]{:S(2)}, u32[]{:S(2)}) collective-permute-start(bf16[14,14,144]{2,1,0:T(8,128)(2,1)} %bitcast.208), channel_id=1, source_target_pairs={{0,8},{8,16},{16,24},{24,32},{32,40},{40,48},{48,56},{56,64},{64,7... | collective-permute-start | bytes 169352 | tf_op jit(solution)/shard_map/ppermute | solution.py:13
  137.6 5.6 %copy-start.13 = (bf16[64,1152]{1,0:T(8,128)(2,1)S(1)}, bf16[64,1152]{1,0:T(8,128)(2,1)}, u32[]{:S(2)}) copy-start(bf16[64,1152]{1,0:T(8,128)(2,1)} %reshape.208) | copy-start | bytes 442372
  143.2 1.4 copy-start.34
  222.9 5.6 %copy-start.1 = (bf16[1152,1024]{1,0:T(8,128)(2,1)S(1)}, bf16[1152,1024]{1,0:T(8,128)(2,1)}, u32[]{:S(2)}) copy-start(bf16[1152,1024]{1,0:T(8,128)(2,1)} %reshape.210) | copy-start | bytes 7077892
  222.9 5.6 %copy-start.37 = (bf16[64]{0:T(256)(128)(2,1)S(1)}, bf16[64]{0:T(256)(128)(2,1)}, u32[]{:S(2)}) copy-start(bf16[64]{0:T(256)(128)(2,1)} %compare_convert_fusion) | copy-start | bytes 388
  222.9 5.6 %copy-start.38 = (f32[64,1152]{1,0:T(8,128)S(1)}, f32[64,1152]{1,0:T(8,128)}, u32[]{:S(2)}) copy-start(f32[64,1152]{1,0:T(8,128)} %get-tuple-element.15) | copy-start | bytes 884740
  226.4 15.7 %copy-start.3 = (f32[2,14,14,144]{3,0,2,1:T(2,128)S(1)}, f32[2,14,14,144]{3,0,2,1:T(2,128)}, u32[]{:S(2)}) copy-start(f32[2,14,14,144]{3,0,2,1:T(2,128)} %get-tuple-element.17) | copy-start | bytes 677380
  226.4 33.1 %copy-start.32 = (bf16[144,288]{1,0:T(8,128)(2,1)S(1)}, bf16[144,288]{1,0:T(8,128)(2,1)}, u32[]{:S(2)}) copy-start(bf16[144,288]{1,0:T(8,128)(2,1)} %param.11) | copy-start | bytes 248836
  226.4 33.1 %copy-start.36 = (f32[2,288]{1,0:T(2,128)S(1)}, f32[2,288]{1,0:T(2,128)}, u32[]{:S(2)}) copy-start(f32[2,288]{1,0:T(2,128)} %copy-done.35) | copy-start | bytes 6916
  226.4 15.5 %collective-permute-start.1 = (bf16[14,14,144]{2,1,0:T(8,128)(2,1)S(1)}, bf16[14,14,144]{2,1,0:T(8,128)(2,1)S(1)}, u32[]{:S(2)}, u32[]{:S(2)}) collective-permute-start(bf16[14,14,144]{2,1,0:T(8,128)(2,1)S(1)} %fusion.31), channel_id=1, source_target_pairs={{8,0},{16,8},{24,16},{32,24},{40,32},{48,40},{56,48},{64,56},{72,6... | collective-permute-start | bytes 169352 | tf_op jit(solution)/shard_map/ppermute | solution.py:13
  229.1 31.1 %copy-start.2 = (f32[2,14,14,3,48]{4,2,1,0,3:T(8,128)S(1)}, f32[2,14,14,3,48]{4,2,1,0,3:T(8,128)}, u32[]{:S(2)}) copy-start(f32[2,14,14,3,48]{4,2,1,0,3:T(8,128)} %get-tuple-element.41) | copy-start | bytes 677380
  230.7 62.5 %all-to-all-start.1 = ((bf16[64,2,512]{2,1,0:T(2,128)(2,1)}), bf16[64,2,512]{2,1,0:T(2,128)(2,1)S(1)}, u32[]{:S(2)}, u32[]{:S(2)}) async-start(bf16[64,2,512]{2,1,0:T(2,128)(2,1)} %reshape.238), calls=%async_computation.1 | async-start | bytes 262144 | tf_op jit(solution)/shard_map/all_to_all | solution.py:141
  241.9 18.8 %copy-start.17 = (bf16[1,144,48]{2,1,0:T(8,128)(2,1)S(1)}, bf16[1,144,48]{2,1,0:T(8,128)(2,1)}, u32[]{:S(2)}) copy-start(bf16[1,144,48]{2,1,0:T(8,128)(2,1)} %copy-done.16) | copy-start | bytes 41476
  242.7 19.1 %copy-start.19 = (bf16[1,144,48]{2,1,0:T(8,128)(2,1)S(1)}, bf16[1,144,48]{2,1,0:T(8,128)(2,1)}, u32[]{:S(2)}) copy-start(bf16[1,144,48]{2,1,0:T(8,128)(2,1)} %copy.236) | copy-start | bytes 41476
  260.1 2.9 copy-start.21
  260.2 3.9 %copy-start.23 = (bf16[1,144,48]{2,1,0:T(8,128)(2,1)S(1)}, bf16[1,144,48]{2,1,0:T(8,128)(2,1)}, u32[]{:S(2)}) copy-start(bf16[1,144,48]{2,1,0:T(8,128)(2,1)} %copy.240) | copy-start | bytes 41476
  260.5 4.7 %copy-start.25 = (bf16[1,144,48]{2,1,0:T(8,128)(2,1)S(1)}, bf16[1,144,48]{2,1,0:T(8,128)(2,1)}, u32[]{:S(2)}) copy-start(bf16[1,144,48]{2,1,0:T(8,128)(2,1)} %copy.243) | copy-start | bytes 41476
  260.8 5.5 %copy-start.27 = (bf16[1,144,48]{2,1,0:T(8,128)(2,1)S(1)}, bf16[1,144,48]{2,1,0:T(8,128)(2,1)}, u32[]{:S(2)}) copy-start(bf16[1,144,48]{2,1,0:T(8,128)(2,1)} %copy.245) | copy-start | bytes 41476
  261.9 4.6 %copy-start.29 = (bf16[1,144,48]{2,1,0:T(8,128)(2,1)S(1)}, bf16[1,144,48]{2,1,0:T(8,128)(2,1)}, u32[]{:S(2)}) copy-start(bf16[1,144,48]{2,1,0:T(8,128)(2,1)} %copy.247) | copy-start | bytes 41476
  263.0 3.8 %copy-start.31 = (bf16[1,144,48]{2,1,0:T(8,128)(2,1)S(1)}, bf16[1,144,48]{2,1,0:T(8,128)(2,1)}, u32[]{:S(2)}) copy-start(bf16[1,144,48]{2,1,0:T(8,128)(2,1)} %copy.249) | copy-start | bytes 41476
  284.9 3.6 %copy-start.4 = (f32[2,14,14,144]{3,0,2,1:T(2,128)S(1)}, f32[2,14,14,144]{3,0,2,1:T(2,128)}, u32[]{:S(2)}) copy-start(f32[2,14,14,144]{3,0,2,1:T(2,128)} %reshape.214) | copy-start | bytes 677380
  285.3 3.1 %copy-start.5 = (f32[2,14,14,144]{3,0,2,1:T(2,128)S(1)}, f32[2,14,14,144]{3,0,2,1:T(2,128)}, u32[]{:S(2)}) copy-start(f32[2,14,14,144]{3,0,2,1:T(2,128)} %reshape.215) | copy-start | bytes 677380
  287.1 2.8 copy-start.6
Sparse Core Ops, SparseCore 0:
  11.3 108.2 all-gather.1
  144.7 78.1 all-reduce.13
